TPU v7x, 32 devices: a whole 2x2x4 slice. The times are simulated.
32 devices in a mesh: cuts: 8 (over z, core), rank: 4 (over y, x).
Axes of the slice: x: 2, y: 2, z: 4, core: 2. Of those that a mesh axis runs over, the one named last changes fastest.
Arguments:
- core_one: float32 [512, 320, 512], P('rank', 'cuts'), may hold values from -6 to 6
- core_two: float32 [512, 320, 512], P('rank', 'cuts'), may hold values from -0.25 to 0.25
- right_sketch: float32 [512, 128], replicated, may hold values from -0.25 to 0.25
- sketch_core: float32 [128, 320, 128], P(None, 'cuts'), may hold values from -0.03125 to 0.03125
Outputs:
- left_core: float32 [512, 320, 128], P('rank', 'cuts')
- middle_core: float32 [128, 320, 128], P('rank', 'cuts')
- carry: float32 [128, 512], replicated
All inputs are finite; a program needn't handle non-finite values.
Results may differ from a plain program's by a relative error of at most 0.00015.
Values sent between devices are 32-bit elements; how exact they have to be, the bound alone decides.
No kernel may reach another device: no remote copies, remote signals or barrier semaphores. Data moves between devices by JAX's collectives and lax.ppermute only.
A program may use at most 128 MiB of HBM per device.

v0:
```python
import jax
import jax.numpy as jnp
from jax import lax
from jax.experimental import pallas as pl
from jax.experimental.pallas import tpu as pltpu
from jax.sharding import PartitionSpec as P

HIGHEST = lax.Precision.HIGHEST
NT = (((1,), (1,)), ((), ()))
NN = (((1,), (0,)), ((), ()))
TN = (((0,), (0,)), ((), ()))
VMEM_LIMIT = 56 * 1024 * 1024
BLOCK = 8


def call(kernel, flops, size, **more):
    return pl.pallas_call(
        kernel,
        compiler_params=pltpu.CompilerParams(vmem_limit_bytes=VMEM_LIMIT),
        cost_estimate=pl.CostEstimate(flops=flops, bytes_accessed=size, transcendentals=0),
        **more,
    )


def shape(*extent):
    return jax.ShapeDtypeStruct(extent, jnp.float32)


def split(value):
    high = value.astype(jnp.bfloat16)
    return high, (value - high.astype(jnp.float32)).astype(jnp.bfloat16)


def mxu(a, b, form):
    return lax.dot_general(a, b, form, preferred_element_type=jnp.float32)


def both_parts(value, axis):
    return jnp.concatenate(split(value), axis=axis)


def fold(value, axis):
    half = value.shape[axis] // 2
    return lax.slice_in_dim(value, 0, half, axis=axis) + lax.slice_in_dim(value, half, 2 * half, axis=axis)


def rows_of(ref):
    return ref.reshape(ref.shape[0] * ref.shape[1], ref.shape[2])


def sketch_kernel(core_ref, right_ref, left_ref, sketched_ref, part_ref, rows_ref):
    local_rows, block, _ = core_ref.shape
    columns = right_ref.shape[1]
    right = both_parts(right_ref[...], 1)
    high, low = split(rows_of(core_ref)[...])
    rows_ref[...] = fold(mxu(high, right, NN) + mxu(low, right, NN), 1)
    left_rows = rows_of(left_ref)

    @pl.when(pl.program_id(0) == 0)
    def _():
        part_ref[...] = jnp.zeros_like(part_ref)

    total = jnp.zeros(part_ref.shape, jnp.float32)
    for pair in range(0, block, 2):
        sides, lefts = [], []
        for n in (pair, pair + 1):
            rows = rows_ref[pl.ds(n, local_rows, stride=block), :]
            sketched_ref[n] = rows
            sides.append(rows)
            lefts.append(left_rows[pl.ds(n, columns, stride=block), :])
        high, low = split(jnp.concatenate(sides, axis=1))
        left = both_parts(jnp.concatenate(lefts, axis=1), 0)
        total = total + fold(mxu(high, left, NT) + mxu(low, left, NT), 1)
    part_ref[...] += total


def sketch(core_two, right_sketch, sketch_core):
    local_rows, slices, width = core_two.shape
    columns = right_sketch.shape[1]
    return call(
        sketch_kernel,
        2 * core_two.size * columns * 4,
        4 * (core_two.size + 2 * sketch_core.size),
        grid=(slices // BLOCK,),
        in_specs=[
            pl.BlockSpec((local_rows, BLOCK, width), lambda i: (0, i, 0)),
            pl.BlockSpec((width, columns), lambda i: (0, 0)),
            pl.BlockSpec((columns, BLOCK, columns), lambda i: (0, i, 0)),
        ],
        out_specs=[
            pl.BlockSpec((BLOCK, local_rows, columns), lambda i: (i, 0, 0)),
            pl.BlockSpec((local_rows, columns), lambda i: (0, 0)),
        ],
        out_shape=[shape(slices, local_rows, columns), shape(local_rows, columns)],
        scratch_shapes=[pltpu.VMEM((local_rows * BLOCK, columns), jnp.float32)],
    )(core_two, right_sketch, sketch_core)


def square_kernel(core_ref, square_ref, same_ref, cross_ref):
    step = pl.program_id(0)
    high, low = split(core_ref[...])

    @pl.when(step == 0)
    def _():
        same_ref[...] = jnp.zeros_like(same_ref)
        cross_ref[...] = jnp.zeros_like(cross_ref)

    same_ref[...] += mxu(high, high, TN)
    cross_ref[...] += mxu(high, low, TN)

    @pl.when(step == pl.num_programs(0) - 1)
    def _():
        cross = cross_ref[...]
        square_ref[...] = same_ref[...] + cross + cross.T


def square_of(flat_one):
    rows, width = flat_one.shape
    block = rows // 10
    return call(
        square_kernel,
        4 * rows * width * width,
        4 * flat_one.size,
        grid=(10,),
        in_specs=[pl.BlockSpec((block, width), lambda i: (i, 0))],
        out_specs=pl.BlockSpec((width, width), lambda i: (0, 0)),
        out_shape=shape(width, width),
        scratch_shapes=[pltpu.VMEM((width, width), jnp.float32)] * 2,
    )(flat_one)


def loose_kernel(raw_ref, *refs):
    block_refs, out_ref = refs[:-1], refs[-1]
    count, local_rows, columns = block_refs[0].shape
    raw = both_parts(raw_ref[...], 1)
    for n in range(count):
        high, low = split(jnp.concatenate([ref[n] for ref in block_refs], axis=0))
        out_ref[n] = fold(mxu(raw, high, TN) + mxu(raw, low, TN), 0)


def loosen(raw, blocks):
    count, local_rows, columns = blocks[0].shape
    return call(
        loose_kernel,
        8 * raw.size * count * columns,
        4 * raw.size + 4 * len(blocks) * blocks[0].size,
        out_shape=shape(count, raw.shape[1], columns),
    )(raw, *blocks)


def carry_kernel(everyone_ref, weight_ref, core_ref, raw_ref, middle_ref, rows_ref, sum_ref):
    step = pl.program_id(0)
    block, columns, _ = everyone_ref.shape
    local_rows = core_ref.shape[0]
    band = middle_ref.shape[0]
    weight_high, weight_low = split(weight_ref[...])
    everyone = jnp.concatenate([everyone_ref[n] for n in range(block)], axis=1)
    high, low = split(everyone)
    spread = mxu(weight_high, high, NN) + mxu(weight_high, low, NN) + mxu(weight_low, high, NN)
    middle_rows = rows_of(middle_ref)
    for n in range(block):
        piece = lax.slice_in_dim(spread, n * columns, (n + 1) * columns, axis=1)
        rows_ref[pl.ds(n, local_rows, stride=block), :] = piece[:local_rows]
        middle_rows[pl.ds(n, band, stride=block), :] = piece[local_rows:]
    rows = both_parts(rows_ref[...], 1)
    high, low = split(rows_of(core_ref)[...])

    @pl.when(step == 0)
    def _():
        sum_ref[...] = jnp.zeros_like(sum_ref)

    total = fold(mxu(rows, high, TN) + mxu(rows, low, TN), 0)
    sum_ref[...] += total

    @pl.when(step == pl.num_programs(0) - 1)
    def _():
        raw_ref[...] = sum_ref[...].T


def carry_rows(everyone, weight, core_two, band):
    local_rows, slices, width = core_two.shape
    columns = everyone.shape[2]
    return call(
        carry_kernel,
        2 * core_two.size * columns * 4,
        4 * core_two.size + 4 * everyone.size,
        grid=(slices // BLOCK,),
        in_specs=[
            pl.BlockSpec((BLOCK, columns, columns), lambda i: (i, 0, 0)),
            pl.BlockSpec((local_rows + band, columns), lambda i: (0, 0)),
            pl.BlockSpec((local_rows, BLOCK, width), lambda i: (0, i, 0)),
        ],
        out_specs=[
            pl.BlockSpec((width, columns), lambda i: (0, 0)),
            pl.BlockSpec((band, BLOCK, columns), lambda i: (0, i, 0)),
        ],
        out_shape=[shape(width, columns), shape(band, slices, columns)],
        scratch_shapes=[
            pltpu.VMEM((local_rows * BLOCK, columns), jnp.float32),
            pltpu.VMEM((columns, width), jnp.float32),
        ],
    )(everyone, weight, core_two)


def apply_kernel(rows_ref, weight_ref, out_ref):
    weight = both_parts(weight_ref[...], 1)
    high, low = split(rows_ref[...])
    out_ref[...] = fold(mxu(high, weight, NN) + mxu(low, weight, NN), 1)


def apply_to(rows, weight, steps):
    count, width = rows.shape
    columns = weight.shape[1]
    return call(
        apply_kernel,
        8 * rows.size * columns,
        4 * (rows.size + count * columns),
        grid=(steps,),
        in_specs=[
            pl.BlockSpec((count // steps, width), lambda i: (i, 0)),
            pl.BlockSpec((width, columns), lambda i: (0, 0)),
        ],
        out_specs=pl.BlockSpec((count // steps, columns), lambda i: (i, 0)),
        out_shape=shape(count, columns),
    )(rows, weight)


def axis_bits(axis):
    return [(axis, bit) for bit in range((lax.axis_size(axis) - 1).bit_length())]


def swap(value, step):
    axis, bit = step
    pairs = [(i, i ^ (1 << bit)) for i in range(lax.axis_size(axis))]
    return lax.ppermute(value, axis, pairs)


def side(step):
    axis, bit = step
    return lax.rem(lax.div(lax.axis_index(axis), 1 << bit), 2)


def halve(value, step):
    half = value.shape[0] // 2
    own = side(step)
    keep = lax.dynamic_slice_in_dim(value, own * half, half, 0)
    give = lax.dynamic_slice_in_dim(value, (1 - own) * half, half, 0)
    return keep + swap(give, step)


def double(value, step):
    other = swap(value, step)
    own = side(step) == 0
    return jnp.concatenate([jnp.where(own, value, other), jnp.where(own, other, value)], axis=0)


def scatter_sum(value, steps):
    for step in steps:
        value = halve(value, step)
    return value


def gather(value, steps):
    for step in reversed(steps):
        value = double(value, step)
    return value


def total(value, steps):
    for step in steps:
        value = value + swap(value, step)
    return value


def exchange(value, axes):
    return lax.all_to_all(value, axes, 0, 0, tiled=True)


def split_sum(value, axes):
    parts = lax.axis_size(axes)
    blocks = value.reshape((parts, value.shape[0] // parts) + value.shape[1:])
    return jnp.sum(exchange(blocks, axes), axis=0)


def gather_all(value, axes):
    parts = lax.axis_size(axes)
    return exchange(jnp.broadcast_to(value[None], (parts,) + value.shape), axes)


def invert_factor(gram):
    factor = jnp.linalg.cholesky(gram)
    unit = jnp.eye(gram.shape[0], dtype=jnp.float32)
    return lax.linalg.triangular_solve(factor, unit, left_side=True, lower=True)


def dot(a, b, contract, precision=HIGHEST):
    return lax.dot_general(
        a, b, (contract, ((), ())), precision=precision, preferred_element_type=jnp.float32
    )


def on_device(core_one, core_two, right_sketch, sketch_core):
    local_rows, slices, width = core_one.shape
    sketch_width = right_sketch.shape[1]
    ranks, cuts = lax.axis_size("rank"), lax.axis_size("cuts")
    rank = lax.axis_index("rank")
    band = sketch_width // ranks
    cut_steps, rank_steps = axis_bits("cuts"), axis_bits("rank")
    steps = cut_steps[:1] + rank_steps + cut_steps[1:]
    both = ("cuts", "rank")
    share = -(-slices // ranks)

    filler = ((0, 0), (0, -slices % BLOCK), (0, 0))
    core_two, sketch_core = jnp.pad(core_two, filler), jnp.pad(sketch_core, filler)
    sketched, part = sketch(core_two, right_sketch, sketch_core)
    sketched = sketched[:slices]
    bridge = gather_all(split_sum(part, "cuts"), both)
    bridge = bridge.reshape(cuts, ranks, -1, sketch_width).swapaxes(0, 1).reshape(width, sketch_width)

    padded = jnp.pad(sketched, ((0, share * ranks - slices), (0, 0), (0, 0)))
    blocks = []
    for offset in range(ranks):
        block = lax.dynamic_slice_in_dim(padded, (rank ^ offset) * share, share, 0)
        if offset:
            block = lax.ppermute(block, "rank", [(i, i ^ offset) for i in range(ranks)])
        blocks.append(block)

    flat_one = core_one.reshape(local_rows * slices, width)
    square = square_of(flat_one)
    square = square.reshape(cuts // 2, 2, ranks, -1, width)
    square = square.transpose(1, 2, 0, 3, 4).reshape(2 * ranks, cuts // 2, -1, width)
    square = scatter_sum(square, cut_steps[:1] + rank_steps[::-1])[0]
    groups = [list(range(core, cuts, 2)) for core in range(2)]
    own_square = jnp.sum(lax.all_to_all(square, "cuts", 0, 0, axis_index_groups=groups, tiled=True), axis=0)
    raw_rows = dot(own_square, bridge, ((1,), (0,)))
    raw = gather_all(raw_rows, both).reshape(width, sketch_width)
    gram = dot(bridge, raw, ((0,), (0,)))

    order = [lax.dynamic_slice_in_dim(raw, (rank ^ i) * local_rows, local_rows, 0) for i in range(ranks)]
    loose = loosen(jnp.concatenate(order, axis=0), blocks)
    first = share // 2
    pieces = []
    for piece, order in ((loose[:first], rank_steps), (loose[first:], rank_steps[::-1])):
        if piece.shape[0]:
            count = piece.shape[0]
            piece = piece[None]
            for step in order:
                piece = double(piece, step)
            if order is not rank_steps:
                bits = len(rank_steps)
                piece = piece.reshape((2,) * bits + piece.shape[1:])
                piece = piece.transpose(tuple(range(bits))[::-1] + tuple(range(bits, bits + 3)))
                piece = piece.reshape((ranks, count) + piece.shape[bits + 1:])
            pieces.append(piece)
    everyone = jnp.concatenate(pieces, axis=1)
    everyone = everyone.reshape((ranks * share,) + everyone.shape[2:])[:slices]

    inverse = invert_factor(gram)
    tight = jnp.einsum("bd,ndc->nbc", inverse, loose, precision=HIGHEST)
    flat_tight = tight.reshape(share * sketch_width, sketch_width)
    second_gram = total(dot(flat_tight, flat_tight, ((0,), (0,))), steps)
    second_inverse = invert_factor(second_gram)

    scale = jnp.sqrt(jnp.float32(local_rows * ranks * slices * cuts))
    solve = scale * dot(bridge, inverse, ((1,), (1,)))
    left_core = apply_to(flat_one, solve, 5).reshape(local_rows, slices, sketch_width)

    own_raw = lax.dynamic_slice_in_dim(raw, rank * local_rows, local_rows, 0)
    weight = dot(dot(own_raw, inverse, ((1,), (1,))), inverse, ((1,), (0,)))
    own_inverse = lax.dynamic_slice_in_dim(inverse, rank * band, band, 0)
    weight = jnp.concatenate([weight, own_inverse], axis=0)
    everyone = jnp.pad(everyone, ((0, -slices % BLOCK), (0, 0), (0, 0)))
    second_raw, rows = carry_rows(everyone, weight, core_two, band)
    second_raw = split_sum(second_raw, both)
    second_raw = gather_all(second_raw, both).reshape(width, sketch_width)
    carry = dot(second_inverse, second_raw, ((1,), (1,)))

    scale = jnp.sqrt(jnp.float32(sketch_width * slices * cuts))
    rows = rows[:, :slices].reshape(band * slices, sketch_width)
    middle_core = scale * dot(rows, second_inverse, ((1,), (1,)))
    middle_core = middle_core.reshape(band, slices, sketch_width)
    return (left_core, middle_core, carry)


def solution(mesh):
    placed = (P("rank", "cuts", None), P("rank", "cuts", None), P(), P(None, "cuts", None))
    return jax.shard_map(
        on_device,
        mesh=mesh,
        in_specs=placed,
        out_specs=(P("rank", "cuts", None), P("rank", "cuts", None), P()),
        check_vma=False,
    )
```

profile of v0, /device:TPU:0, one launch (start us, length us, event | category | flops | bytes accessed | tf_op | source)
XLA Modules:
  0.0 212.0 jit_solution(12774692545425994218)
XLA Ops:
  0.6 13.4 %shard_map.68 = f32[512,512]{1,0:T(8,128)} custom-call(f32[5120,512]{1,0:T(8,128)} %bitcast.80), custom_call_target="tpu_custom_call" | custom-call | flops 5368709120 | bytes 10485760 | tf_op jit(solution)/shard_map/pallas_call | solution.py:120
  14.0 1.1 constant_dynamic-slice_fusion.11
  15.6 1.5 collective-permute-done
  17.1 1.1 dynamic-slice_add_fusion
  18.3 0.7 constant_dynamic-slice_fusion.10
  19.0 2.9 %collective-permute-start.1 = (f32[2,4,16,512]{3,2,0,1:T(8,128)}, f32[2,4,16,512]{3,2,0,1:T(8,128)}, u32[]{:S(2)}, u32[]{:S(2)}) collective-permute-start(f32[2,4,16,512]{3,2,0,1:T(8,128)} %constant_dynamic-slice_fusion.10), channel_id=1, source_target_pairs={{0,2},{1,3},{2,0},{3,1},{4,6},{5,7},{6,4},{7,5},{8,10},{9,11},{10,... | collective-permute-start | bytes 786440 | tf_op jit(solution)/shard_map/ppermute | solution.py:235
  21.9 10.9 %shard_map.67 = (f32[40,128,128]{2,1,0:T(8,128)}, f32[128,128]{1,0:T(8,128)}) custom-call(f32[128,40,512]{2,1,0:T(8,128)} %core_ref.3, f32[512,128]{1,0:T(8,128)} %right_ref.1, f32[128,40,128]{2,1,0:T(8,128)} %left_ref.1), custom_call_target="tpu_custom_call" | custom-call | flops 2684354560 | bytes 15728640 | tf_op jit(solution)/shard_map/pallas_call | solution.py:80
  32.8 5.2 %all-to-all-start = ((f32[8,16,128]{2,1,0:T(8,128)}), f32[8,16,128]{2,1,0:T(8,128)S(1)}, u32[]{:S(2)}, u32[]{:S(2)}) async-start(f32[8,16,128]{2,1,0:T(8,128)} %bitcast.98), calls=%async_computation | async-start | bytes 131072 | tf_op jit(solution)/shard_map/all_to_all | solution.py:276
  37.9 5.9 %all-to-all-done = f32[8,16,128]{2,1,0:T(8,128)S(1)} async-done(((f32[8,16,128]{2,1,0:T(8,128)}), f32[8,16,128]{2,1,0:T(8,128)S(1)}, u32[]{:S(2)}, u32[]{:S(2)}) %all-to-all-start) | async-done | bytes 65568 | tf_op jit(solution)/shard_map/all_to_all | solution.py:276
  43.9 0.7 broadcast_in_dim.10
  44.6 2.6 %all-to-all-start.1 = ((f32[32,16,128]{2,1,0:T(8,128)}), f32[32,16,128]{2,1,0:T(8,128)S(1)}, u32[]{:S(2)}, u32[]{:S(2)}) async-start(f32[32,16,128]{2,1,0:T(8,128)} %broadcast_in_dim.10), calls=%async_computation.1 | async-start | bytes 524288 | tf_op jit(solution)/shard_map/all_to_all | solution.py:276
  47.2 1.0 dynamic-slice_add_fusion.1
  48.2 0.7 copy-done.3
  48.9 1.7 collective-permute-start.2
  50.6 5.3 %collective-permute-done.2 = f32[1,4,16,512]{3,2,0,1:T(8,128)S(1)} collective-permute-done((f32[1,4,16,512]{3,2,0,1:T(8,128)S(1)}, f32[1,4,16,512]{3,2,0,1:T(8,128)S(1)}, u32[]{:S(2)}, u32[]{:S(2)}) %collective-permute-start.2) | collective-permute-done | bytes 131104 | tf_op jit(solution)/shard_map/ppermute | solution.py:235
  55.9 1.6 add_bitcast_fusion
  57.4 0.7 all-to-all-done.1
  58.1 3.9 %all-to-all-start.2 = ((f32[4,16,512]{2,1,0:T(8,128)}), f32[4,16,512]{2,1,0:T(8,128)S(1)}, u32[]{:S(2)}, u32[]{:S(2)}) async-start(f32[4,16,512]{2,1,0:T(8,128)} %add_bitcast_fusion), calls=%async_computation.2 | async-start | bytes 262144 | tf_op jit(solution)/shard_map/all_to_all | solution.py:334
  62.0 1.0 copy.19
  63.0 5.1 %all-to-all-done.2 = f32[4,16,512]{2,1,0:T(8,128)S(1)} async-done(((f32[4,16,512]{2,1,0:T(8,128)}), f32[4,16,512]{2,1,0:T(8,128)S(1)}, u32[]{:S(2)}, u32[]{:S(2)}) %all-to-all-start.2) | async-done | bytes 131104 | tf_op jit(solution)/shard_map/all_to_all | solution.py:334
  68.4 0.7 broadcast_in_dim.12
  69.1 3.2 %all-to-all-start.3 = ((f32[32,16,128]{2,1,0:T(8,128)}), f32[32,16,128]{2,1,0:T(8,128)S(1)}, u32[]{:S(2)}, u32[]{:S(2)}) async-start(f32[32,16,128]{2,1,0:T(8,128)} %broadcast_in_dim.12), calls=%async_computation.3 | async-start | bytes 524288 | tf_op jit(solution)/shard_map/all_to_all | solution.py:276
  72.3 1.6 constant_dynamic-slice_fusion.1
  73.9 1.8 collective-permute-start.3
  75.7 1.5 collective-permute-start.4
  77.4 5.8 %all-to-all-done.3 = f32[32,16,128]{2,1,0:T(8,128)S(1)} async-done(((f32[32,16,128]{2,1,0:T(8,128)}), f32[32,16,128]{2,1,0:T(8,128)S(1)}, u32[]{:S(2)}, u32[]{:S(2)}) %all-to-all-start.3) | async-done | bytes 262176 | tf_op jit(solution)/shard_map/all_to_all | solution.py:276
  83.2 0.6 fusion.12
  83.9 11.7 %cholesky.44 = f32[128,128]{1,0:T(8,128)S(1)} custom-call(f32[128,128]{1,0:T(8,128)S(1)} %fusion.10), custom_call_target="Cholesky" | custom-call | tf_op jit(solution)/shard_map/jit(cholesky)/cholesky | solution.py:291
  95.7 0.6 compare_reduce_fusion.1
  96.3 0.7 fusion.4
  97.0 9.8 %custom-call.6 = f32[1,128,128]{1,2,0:T(8,128)S(1)} custom-call(f32[1,128,128]{2,1,0:T(8,128)S(1)} %fusion.4), custom_call_target="InvertDiagBlocksLowerTriangular" | custom-call | tf_op jit(solution)/shard_map/triangular_solve/custom-call.0 | solution.py:293
  106.8 0.7 pad_maximum_fusion.4.raw_ref
  107.9 0.8 copy-done.4
  109.1 4.2 %shard_map.70 = f32[10,128,128]{2,1,0:T(8,128)} custom-call(f32[512,128]{1,0:T(8,128)} %pad_maximum_fusion.4.raw_ref, f32[10,128,128]{2,1,0:T(8,128)} %get-tuple-element.16.refs_0_, f32[10,128,128]{2,1,0:T(8,128)} %copy-done.4, f32[10,128,128]{2,1,0:T(8,128)} %copy-done.5, f32[10,128,128]{2,1,0:T(8,128)} %copy-done.6), custom_call_target="tpu_custom_call" | custom-call | flops 671088640 | bytes 2883584 | tf_op jit(solution)/shard_map/pallas_call | solution.py:143
  113.3 1.2 slice_bitcast_fusion.1
  114.5 2.3 %convolution_bitcast_fusion = f32[10,128,128]{1,2,0:T(8,128)S(1)} fusion(f32[10,128,128]{2,1,0:T(8,128)} %shard_map.70, f32[128,128]{1,0:T(8,128)S(1)} %fusion.2), kind=kOutput, calls=%fused_computation.3 | convolution fusion | flops 251658240 | bytes 1376256 | tf_op jit(solution)/shard_map/bd,ndc->nbc/dot_general | solution.py:359
  116.8 0.6 collective-permute-start.6
  117.3 0.9 collective-permute-start.8
  118.2 0.7 convolution_bitcast_fusion.1
  119.0 1.1 convolution_multiply_fusion.1.weight_ref
  120.0 5.5 %collective-permute-done.6 = f32[1,5,128,128]{3,2,1,0:T(8,128)S(1)} collective-permute-done((f32[1,5,128,128]{3,2,1,0:T(8,128)S(1)}, f32[1,5,128,128]{3,2,1,0:T(8,128)S(1)}, u32[]{:S(2)}, u32[]{:S(2)}) %collective-permute-start.6) | collective-permute-done | bytes 327712 | tf_op jit(solution)/shard_map/ppermute | solution.py:235
  125.5 0.9 collective-permute-done.8
  126.6 0.9 collective-permute-start.7
  127.5 1.5 collective-permute-start.9
  129.3 0.6 collective-permute-start.11
  130.4 13.6 %collective-permute-done.11 = f32[128,128]{0,1:T(8,128)S(1)} collective-permute-done((f32[128,128]{0,1:T(8,128)S(1)}, f32[128,128]{0,1:T(8,128)S(1)}, u32[]{:S(2)}, u32[]{:S(2)}) %collective-permute-start.11) | collective-permute-done | bytes 65568 | tf_op jit(solution)/shard_map/ppermute | solution.py:235
  144.0 1.2 collective-permute-start.12
  145.3 3.1 %collective-permute-done.12 = f32[128,128]{0,1:T(8,128)S(1)} collective-permute-done((f32[128,128]{0,1:T(8,128)S(1)}, f32[128,128]{0,1:T(8,128)S(1)}, u32[]{:S(2)}, u32[]{:S(2)}) %collective-permute-start.12) | collective-permute-done | bytes 65568 | tf_op jit(solution)/shard_map/ppermute | solution.py:235
  148.4 0.7 collective-permute-start.13
  149.0 0.6 pad_maximum_fusion.5.weight_ref
  149.7 3.7 %collective-permute-done.13 = f32[128,128]{0,1:T(8,128)S(1)} collective-permute-done((f32[128,128]{0,1:T(8,128)S(1)}, f32[128,128]{0,1:T(8,128)S(1)}, u32[]{:S(2)}, u32[]{:S(2)}) %collective-permute-start.13) | collective-permute-done | bytes 65568 | tf_op jit(solution)/shard_map/ppermute | solution.py:235
  153.4 0.6 collective-permute-start.14
  154.5 1.8 pad_maximum_fusion
  156.2 10.9 %shard_map.71 = (f32[512,128]{1,0:T(8,128)}, f32[32,40,128]{2,1,0:T(8,128)}) custom-call(f32[40,128,128]{2,1,0:T(8,128)} %bitcast.82, f32[160,128]{1,0:T(8,128)} %pad_maximum_fusion.5.weight_ref, f32[128,40,512]{2,1,0:T(8,128)} %core_ref.3), custom_call_target="tpu_custom_call" | custom-call | flops 2684354560 | bytes 13107200 | tf_op jit(solution)/shard_map/pallas_call | solution.py:183
  167.1 3.6 %all-to-all-start.4 = ((f32[32,16,128]{2,1,0:T(8,128)}), f32[32,16,128]{2,1,0:T(8,128)S(1)}, u32[]{:S(2)}, u32[]{:S(2)}) async-start(f32[32,16,128]{2,1,0:T(8,128)} %bitcast.97), calls=%async_computation.4 | async-start | bytes 524288 | tf_op jit(solution)/shard_map/all_to_all | solution.py:276
  170.8 8.6 %shard_map.69 = f32[5120,128]{1,0:T(8,128)} custom-call(f32[5120,512]{1,0:T(8,128)} %bitcast.81, f32[512,128]{1,0:T(8,128)} %convolution_multiply_fusion.1.weight_ref), custom_call_target="tpu_custom_call" | custom-call | flops 2684354560 | bytes 13107200 | tf_op jit(solution)/shard_map/pallas_call | solution.py:214
  179.5 11.7 %cholesky.55 = f32[128,128]{1,0:T(8,128)S(1)} custom-call(f32[128,128]{1,0:T(8,128)S(1)} %fusion.7), custom_call_target="Cholesky" | custom-call | tf_op jit(solution)/shard_map/jit(cholesky)/cholesky | solution.py:291
  191.2 0.7 compare_reduce_fusion
  192.0 0.7 broadcast_in_dim.15
  192.7 5.8 %all-to-all-start.5 = ((f32[32,16,128]{2,1,0:T(8,128)}), f32[32,16,128]{2,1,0:T(8,128)S(1)}, u32[]{:S(2)}, u32[]{:S(2)}) async-start(f32[32,16,128]{2,1,0:T(8,128)} %broadcast_in_dim.15), calls=%async_computation.5 | async-start | bytes 524288 | tf_op jit(solution)/shard_map/all_to_all | solution.py:276
  198.6 0.7 fusion.5
  199.3 9.8 %custom-call.7 = f32[1,128,128]{1,2,0:T(8,128)S(1)} custom-call(f32[1,128,128]{2,1,0:T(8,128)S(1)} %fusion.5), custom_call_target="InvertDiagBlocksLowerTriangular" | custom-call | tf_op jit(solution)/shard_map/triangular_solve/custom-call.0 | solution.py:293
  209.4 1.5 convolution_multiply_fusion
  210.9 1.1 fusion.15
  (55 shorter events, 3.9 us)
Async XLA Ops:
  15.1 2.1 collective-permute-start
  19.0 28.2 %collective-permute-start.1 = (f32[2,4,16,512]{3,2,0,1:T(8,128)}, f32[2,4,16,512]{3,2,0,1:T(8,128)}, u32[]{:S(2)}, u32[]{:S(2)}) collective-permute-start(f32[2,4,16,512]{3,2,0,1:T(8,128)} %constant_dynamic-slice_fusion.10), channel_id=1, source_target_pairs={{0,2},{1,3},{2,0},{3,1},{4,6},{5,7},{6,4},{7,5},{8,10},{9,11},{10,... | collective-permute-start | bytes 786440 | tf_op jit(solution)/shard_map/ppermute | solution.py:235
  32.8 39.6 %copy-start.1 = (f32[40,128,128]{2,1,0:T(8,128)S(1)}, f32[40,128,128]{2,1,0:T(8,128)}, u32[]{:S(2)}) copy-start(f32[40,128,128]{2,1,0:T(8,128)} %get-tuple-element.10) | copy-start | bytes 7864324
  32.8 11.1 %all-to-all-start = ((f32[8,16,128]{2,1,0:T(8,128)}), f32[8,16,128]{2,1,0:T(8,128)S(1)}, u32[]{:S(2)}, u32[]{:S(2)}) async-start(f32[8,16,128]{2,1,0:T(8,128)} %bitcast.98), calls=%async_computation | async-start | bytes 131072 | tf_op jit(solution)/shard_map/all_to_all | solution.py:276
  44.6 13.5 %all-to-all-start.1 = ((f32[32,16,128]{2,1,0:T(8,128)}), f32[32,16,128]{2,1,0:T(8,128)S(1)}, u32[]{:S(2)}, u32[]{:S(2)}) async-start(f32[32,16,128]{2,1,0:T(8,128)} %broadcast_in_dim.10), calls=%async_computation.1 | async-start | bytes 524288 | tf_op jit(solution)/shard_map/all_to_all | solution.py:276
  48.2 0.7 copy-start.3
  48.9 7.0 %collective-permute-start.2 = (f32[1,4,16,512]{3,2,0,1:T(8,128)S(1)}, f32[1,4,16,512]{3,2,0,1:T(8,128)S(1)}, u32[]{:S(2)}, u32[]{:S(2)}) collective-permute-start(f32[1,4,16,512]{3,2,0,1:T(8,128)S(1)} %constant_dynamic-slice_fusion.9), channel_id=1, source_target_pairs={{0,1},{1,0},{2,3},{3,2},{4,5},{5,4},{6,7},{7,6},{8,9},{9,8},{10,11... | collective-permute-start | bytes 393224 | tf_op jit(solution)/shard_map/ppermute | solution.py:235
  58.1 3.9 %copy-start.2 = (f32[32,16,128]{2,1,0:T(8,128)}, f32[32,16,128]{2,1,0:T(8,128)S(1)}, u32[]{:S(2)}) copy-start(f32[32,16,128]{2,1,0:T(8,128)S(1)} %all-to-all-done.1) | copy-start | bytes 786436
  58.1 10.0 %all-to-all-start.2 = ((f32[4,16,512]{2,1,0:T(8,128)}), f32[4,16,512]{2,1,0:T(8,128)S(1)}, u32[]{:S(2)}, u32[]{:S(2)}) async-start(f32[4,16,512]{2,1,0:T(8,128)} %add_bitcast_fusion), calls=%async_computation.2 | async-start | bytes 262144 | tf_op jit(solution)/shard_map/all_to_all | solution.py:334
  69.1 14.1 %all-to-all-start.3 = ((f32[32,16,128]{2,1,0:T(8,128)}), f32[32,16,128]{2,1,0:T(8,128)S(1)}, u32[]{:S(2)}, u32[]{:S(2)}) async-start(f32[32,16,128]{2,1,0:T(8,128)} %broadcast_in_dim.12), calls=%async_computation.3 | async-start | bytes 524288 | tf_op jit(solution)/shard_map/all_to_all | solution.py:276
  73.9 33.9 %collective-permute-start.3 = (f32[10,128,128]{2,1,0:T(8,128)}, f32[10,128,128]{2,1,0:T(8,128)S(1)}, u32[]{:S(2)}, u32[]{:S(2)}) collective-permute-start(f32[10,128,128]{2,1,0:T(8,128)} %get-tuple-element.15), channel_id=1, source_target_pairs={{0,1},{1,0},{2,3},{3,2},{4,5},{5,4},{6,7},{7,6},{8,9},{9,8},{10,11... | collective-permute-start | bytes 1966088 | tf_op jit(solution)/shard_map/ppermute | solution.py:325
  75.7 32.2 %collective-permute-start.4 = (f32[10,128,128]{2,1,0:T(8,128)}, f32[10,128,128]{2,1,0:T(8,128)S(1)}, u32[]{:S(2)}, u32[]{:S(2)}) collective-permute-start(f32[10,128,128]{2,1,0:T(8,128)} %get-tuple-element.14), channel_id=1, source_target_pairs={{0,2},{1,3},{2,0},{3,1},{4,6},{5,7},{6,4},{7,5},{8,10},{9,11},{10,... | collective-permute-start | bytes 1966088 | tf_op jit(solution)/shard_map/ppermute | solution.py:325
  77.1 30.7 %collective-permute-start.5 = (f32[10,128,128]{2,1,0:T(8,128)}, f32[10,128,128]{2,1,0:T(8,128)S(1)}, u32[]{:S(2)}, u32[]{:S(2)}) collective-permute-start(f32[10,128,128]{2,1,0:T(8,128)} %get-tuple-element.13), channel_id=1, source_target_pairs={{0,3},{1,2},{2,1},{3,0},{4,7},{5,6},{6,5},{7,4},{8,11},{9,10},{10,... | collective-permute-start | bytes 1966088 | tf_op jit(solution)/shard_map/ppermute | solution.py:325
  107.8 0.9 copy-start.4
  107.9 1.0 copy-start.5
  107.9 1.2 copy-start.6
  113.3 13.2 %copy-start = (f32[10,128,128]{2,1,0:T(8,128)S(1)}, f32[10,128,128]{2,1,0:T(8,128)}, u32[]{:S(2)}) copy-start(f32[10,128,128]{2,1,0:T(8,128)} %shard_map.70) | copy-start | bytes 1966084
  116.8 8.8 %collective-permute-start.6 = (f32[1,5,128,128]{3,2,1,0:T(8,128)S(1)}, f32[1,5,128,128]{3,2,1,0:T(8,128)S(1)}, u32[]{:S(2)}, u32[]{:S(2)}) collective-permute-start(f32[1,5,128,128]{3,2,1,0:T(8,128)S(1)} %get-tuple-element.27), channel_id=1, source_target_pairs={{0,1},{1,0},{2,3},{3,2},{4,5},{5,4},{6,7},{7,6},{8,9},{9,8},{10,11... | collective-permute-start | bytes 983048 | tf_op jit(solution)/shard_map/ppermute | solution.py:235
  117.3 9.1 %collective-permute-start.8 = (f32[1,5,128,128]{3,2,1,0:T(8,128)S(1)}, f32[1,5,128,128]{3,2,1,0:T(8,128)S(1)}, u32[]{:S(2)}, u32[]{:S(2)}) collective-permute-start(f32[1,5,128,128]{3,2,1,0:T(8,128)S(1)} %get-tuple-element.28), channel_id=1, source_target_pairs={{0,2},{1,3},{2,0},{3,1},{4,6},{5,7},{6,4},{7,5},{8,10},{9,11},{10,... | collective-permute-start | bytes 983048 | tf_op jit(solution)/shard_map/ppermute | solution.py:235
  118.9 10.4 %collective-permute-start.10 = (f32[128,128]{0,1:T(8,128)S(1)}, f32[128,128]{0,1:T(8,128)S(1)}, u32[]{:S(2)}, u32[]{:S(2)}) collective-permute-start(f32[128,128]{0,1:T(8,128)S(1)} %convolution_bitcast_fusion.1), channel_id=1, source_target_pairs={{0,4},{4,0},{8,12},{12,8},{16,20},{20,16},{24,28},{28,24},{1,5},{5... | collective-permute-start | bytes 196616 | tf_op jit(solution)/shard_map/ppermute | solution.py:235
  126.6 27.4 %collective-permute-start.7 = (f32[2,5,128,128]{3,2,1,0:T(8,128)S(1)}, f32[2,5,128,128]{3,2,1,0:T(8,128)S(1)}, u32[]{:S(2)}, u32[]{:S(2)}) collective-permute-start(f32[2,5,128,128]{3,2,1,0:T(8,128)S(1)} %pad_maximum_fusion.2), channel_id=1, source_target_pairs={{0,2},{1,3},{2,0},{3,1},{4,6},{5,7},{6,4},{7,5},{8,10},{9,11},{10,... | collective-permute-start | bytes 1966088 | tf_op jit(solution)/shard_map/ppermute | solution.py:235
  127.5 26.5 %collective-permute-start.9 = (f32[2,5,128,128]{3,2,1,0:T(8,128)S(1)}, f32[2,5,128,128]{3,2,1,0:T(8,128)S(1)}, u32[]{:S(2)}, u32[]{:S(2)}) collective-permute-start(f32[2,5,128,128]{3,2,1,0:T(8,128)S(1)} %pad_maximum_fusion.3), channel_id=1, source_target_pairs={{0,1},{1,0},{2,3},{3,2},{4,5},{5,4},{6,7},{7,6},{8,9},{9,8},{10,11... | collective-permute-start | bytes 1966088 | tf_op jit(solution)/shard_map/ppermute | solution.py:235
  129.3 14.7 %collective-permute-start.11 = (f32[128,128]{0,1:T(8,128)S(1)}, f32[128,128]{0,1:T(8,128)S(1)}, u32[]{:S(2)}, u32[]{:S(2)}) collective-permute-start(f32[128,128]{0,1:T(8,128)S(1)} %add.97), channel_id=1, source_target_pairs={{0,1},{1,0},{2,3},{3,2},{4,5},{5,4},{6,7},{7,6},{8,9},{9,8},{10,11... | collective-permute-start | bytes 196616 | tf_op jit(solution)/shard_map/ppermute | solution.py:235
  144.0 4.3 %collective-permute-start.12 = (f32[128,128]{0,1:T(8,128)S(1)}, f32[128,128]{0,1:T(8,128)S(1)}, u32[]{:S(2)}, u32[]{:S(2)}) collective-permute-start(f32[128,128]{0,1:T(8,128)S(1)} %add.98), channel_id=1, source_target_pairs={{0,2},{1,3},{2,0},{3,1},{4,6},{5,7},{6,4},{7,5},{8,10},{9,11},{10,... | collective-permute-start | bytes 196616 | tf_op jit(solution)/shard_map/ppermute | solution.py:235
  148.4 5.0 %collective-permute-start.13 = (f32[128,128]{0,1:T(8,128)S(1)}, f32[128,128]{0,1:T(8,128)S(1)}, u32[]{:S(2)}, u32[]{:S(2)}) collective-permute-start(f32[128,128]{0,1:T(8,128)S(1)} %add.99), channel_id=1, source_target_pairs={{0,8},{4,12},{8,0},{12,4},{16,24},{20,28},{24,16},{28,20},{1,9},{5... | collective-permute-start | bytes 196616 | tf_op jit(solution)/shard_map/ppermute | solution.py:235
  153.4 26.0 %collective-permute-start.14 = (f32[128,128]{0,1:T(8,128)S(1)}, f32[128,128]{0,1:T(8,128)S(1)}, u32[]{:S(2)}, u32[]{:S(2)}) collective-permute-start(f32[128,128]{0,1:T(8,128)S(1)} %add.100), channel_id=1, source_target_pairs={{0,16},{4,20},{8,24},{12,28},{16,0},{20,4},{24,8},{28,12},{1,17},{... | collective-permute-start | bytes 196616 | tf_op jit(solution)/shard_map/ppermute | solution.py:235
  167.1 24.8 %all-to-all-start.4 = ((f32[32,16,128]{2,1,0:T(8,128)}), f32[32,16,128]{2,1,0:T(8,128)S(1)}, u32[]{:S(2)}, u32[]{:S(2)}) async-start(f32[32,16,128]{2,1,0:T(8,128)} %bitcast.97), calls=%async_computation.4 | async-start | bytes 524288 | tf_op jit(solution)/shard_map/all_to_all | solution.py:276
  170.8 38.6 %copy-start.7 = (f32[32,40,128]{2,1,0:T(8,128)S(1)}, f32[32,40,128]{2,1,0:T(8,128)}, u32[]{:S(2)}) copy-start(f32[32,40,128]{2,1,0:T(8,128)} %get-tuple-element.11) | copy-start | bytes 1966084
  192.7 18.2 %all-to-all-start.5 = ((f32[32,16,128]{2,1,0:T(8,128)}), f32[32,16,128]{2,1,0:T(8,128)S(1)}, u32[]{:S(2)}, u32[]{:S(2)}) async-start(f32[32,16,128]{2,1,0:T(8,128)} %broadcast_in_dim.15), calls=%async_computation.5 | async-start | bytes 524288 | tf_op jit(solution)/shard_map/all_to_all | solution.py:276
where the time goes:
time: 213 us; the launch traced here: 212 us
  other arithmetic  53.3 us (25%)
  waiting for transfers between devices  51.1 us (24%)
  Pallas kernels  47.9 us (22%)
  starting transfers between devices  39.9 us (19%)
  local copies, waits for them, and re-layouts  9.94 us (5%)
  matrix products  8.73 us (4%)
    ppermute x12, waiting for transfers between devices, swap(): return lax.ppermute(value, axis, pairs)  33.6 us
    another operation x6, other arithmetic, invert_factor(): factor = jnp.linalg.cholesky(gram)  24.8 us
    another operation x4, other arithmetic, invert_factor(): return lax.linalg.triangular_solve(factor, unit, left_side=True, lower=True)  21 us
    all_to_all x5, starting transfers between devices, exchange(): return lax.all_to_all(value, axes, 0, 0, tiled=True)  20.4 us
    pallas_call x1, Pallas kernels, square_of(): call(square_kernel, 4 * rows * width * width, 4 * flat_one.size, grid=(10...  13.4 us
    all_to_all x5, waiting for transfers between devices, exchange(): return lax.all_to_all(value, axes, 0, 0, tiled=True)  12.4 us
    ppermute x12, starting transfers between devices, swap(): return lax.ppermute(value, axis, pairs)  12.1 us
    pallas_call x1, Pallas kernels, sketch(): call(sketch_kernel, 2 * core_two.size * columns * 4, 4 * (core_two.size +...  10.9 us
  transfers between devices with their start and end apart: 21, of which 11 were waited for; matrix products, arithmetic and copies ran while one was open for 29% of the time, Pallas kernels for 14%

commit v1 on v0

--- a/solution.py
+++ b/solution.py
@@ -276,6 +276,10 @@
     return lax.all_to_all(value, axes, 0, 0, tiled=True)
 
 
+def split_blocks(blocks, groups):
+    return jnp.sum(lax.all_to_all(blocks, ("cuts", "rank"), 0, 0, axis_index_groups=groups, tiled=True), axis=0)
+
+
 def split_sum(value, axes):
     parts = lax.axis_size(axes)
     blocks = value.reshape((parts, value.shape[0] // parts) + value.shape[1:])
@@ -287,10 +291,68 @@
     return exchange(jnp.broadcast_to(value[None], (parts,) + value.shape), axes)
 
 
+def small_inverse(entry):
+    size = len(entry)
+    entry = [list(row) for row in entry]
+    inverse = [[None] * size for _ in range(size)]
+    for k in range(size):
+        pivot = entry[k][k]
+        root = lax.rsqrt(pivot)
+        root = root * (1.5 - 0.5 * pivot * root * root)
+        inverse[k][k] = root
+        for i in range(k + 1, size):
+            entry[i][k] = entry[i][k] * root
+        for i in range(k + 1, size):
+            for m in range(k + 1, i + 1):
+                entry[i][m] = entry[i][m] - entry[i][k] * entry[m][k]
+    for k in range(size):
+        for i in range(k + 1, size):
+            total = entry[i][k] * inverse[k][k]
+            for m in range(k + 1, i):
+                total = total + entry[i][m] * inverse[m][k]
+            inverse[i][k] = -total * inverse[i][i]
+    return inverse
+
+
+def factor_kernel(gram_ref, inverse_ref):
+    size, tile = gram_ref.shape[0], BLOCK
+    count = size // tile
+    left = [gram_ref[pl.ds(i * tile, tile), :] for i in range(count)]
+    lane = lax.broadcasted_iota(jnp.int32, (tile, size), 1)
+    sublane = lax.broadcasted_iota(jnp.int32, (tile, size), 0)
+    right = [jnp.where(lane == sublane + i * tile, 1.0, 0.0) for i in range(count)]
+
+    def spread(value, row, column):
+        return jnp.broadcast_to(value[row:row + 1, column:column + 1], (tile, size))
+
+    for j in range(count):
+        corner = [[spread(left[j], i, j * tile + k) for k in range(i + 1)] for i in range(tile)]
+        small = small_inverse(corner)
+        columns = []
+        for k in range(tile):
+            column = jnp.where(sublane == k, small[k][k], 0.0)
+            for i in range(k + 1, tile):
+                column = jnp.where(sublane == i, small[i][k], column)
+            columns.append(column)
+        done_left = sum(columns[k] * left[j][k:k + 1, :] for k in range(tile))
+        done_right = sum(columns[k] * right[j][k:k + 1, :] for k in range(tile))
+        inverse_ref[pl.ds(j * tile, tile), :] = done_right
+        if j + 1 < count:
+            turned = done_left.T
+            for i in range(j + 1, count):
+                for k in range(tile):
+                    factor = jnp.broadcast_to(turned[i * tile:(i + 1) * tile, k:k + 1], (tile, size))
+                    left[i] = left[i] - factor * done_left[k:k + 1, :]
+                    right[i] = right[i] - factor * done_right[k:k + 1, :]
+
+
 def invert_factor(gram):
-    factor = jnp.linalg.cholesky(gram)
-    unit = jnp.eye(gram.shape[0], dtype=jnp.float32)
-    return lax.linalg.triangular_solve(factor, unit, left_side=True, lower=True)
+    return call(
+        factor_kernel,
+        4 * gram.size * gram.shape[0],
+        8 * gram.size,
+        out_shape=shape(*gram.shape),
+    )(gram)
 
 
 def dot(a, b, contract, precision=HIGHEST):
@@ -308,6 +370,9 @@
     cut_steps, rank_steps = axis_bits("cuts"), axis_bits("rank")
     steps = cut_steps[:1] + rank_steps + cut_steps[1:]
     both = ("cuts", "rank")
+    core_groups = [
+        [cut * ranks + place for cut in range(core, cuts, 2) for place in range(ranks)] for core in range(2)
+    ]
     share = -(-slices // ranks)
 
     filler = ((0, 0), (0, -slices % BLOCK), (0, 0))
@@ -327,17 +392,17 @@
 
     flat_one = core_one.reshape(local_rows * slices, width)
     square = square_of(flat_one)
-    square = square.reshape(cuts // 2, 2, ranks, -1, width)
-    square = square.transpose(1, 2, 0, 3, 4).reshape(2 * ranks, cuts // 2, -1, width)
-    square = scatter_sum(square, cut_steps[:1] + rank_steps[::-1])[0]
-    groups = [list(range(core, cuts, 2)) for core in range(2)]
-    own_square = jnp.sum(lax.all_to_all(square, "cuts", 0, 0, axis_index_groups=groups, tiled=True), axis=0)
+    square = square.reshape(2, ranks * cuts // 2, -1, width)
+    square = halve(square, cut_steps[0])[0]
+    own_square = split_blocks(square, core_groups)
     raw_rows = dot(own_square, bridge, ((1,), (0,)))
-    raw = gather_all(raw_rows, both).reshape(width, sketch_width)
+    raw = gather_all(raw_rows, both).reshape(cuts // 2, 2, ranks, -1, sketch_width)
+    raw = raw.transpose(1, 0, 2, 3, 4).reshape(width, sketch_width)
     gram = dot(bridge, raw, ((0,), (0,)))
 
     order = [lax.dynamic_slice_in_dim(raw, (rank ^ i) * local_rows, local_rows, 0) for i in range(ranks)]
     loose = loosen(jnp.concatenate(order, axis=0), blocks)
+    gram, loose = lax.optimization_barrier((gram, loose))
     first = share // 2
     pieces = []
     for piece, order in ((loose[:first], rank_steps), (loose[first:], rank_steps[::-1])):

time: 213 us -> 210 us (0.986)
  other arithmetic: 53.3 us -> 7.5 us
  waiting for transfers between devices: 51.1 us -> 72.3 us
  Pallas kernels: 47.9 us -> 63.5 us
  blocking collectives: 0 us -> 11.9 us
  starting transfers between devices: 39.9 us -> 33.5 us
    another operation x10 -> x0, other arithmetic: 45.8 us -> none  [the longest x6 24.8 us: invert_factor(): factor = jnp.linalg.cholesky(gram)]
    ppermute x3, waiting for transfers between devices: 0.01 us -> 22.1 us  [on_device(): block = lax.ppermute(block, 'rank', [(i, i ^ offset) for i in range(ranks)])]
    pallas_call x0 -> x2, Pallas kernels: none -> 15.5 us  [invert_factor(): call(factor_kernel, 4 * gram.size * gram.shape[0], 8 * gram.size, out_sha...]
    ppermute x12 -> x10, waiting for transfers between devices: 33.6 us -> 21.6 us  [swap(): return lax.ppermute(value, axis, pairs)]
    all_to_all x0 -> x1, blocking collectives: none -> 11.9 us  [exchange(): return lax.all_to_all(value, axes, 0, 0, tiled=True)]
    all_to_all x1, waiting for transfers between devices: 5.1 us -> 13.7 us  [split_blocks(): lax.all_to_all(blocks, ('cuts', 'rank'), 0, 0, axis_index_groups=groups,...]
    all_to_all x5 -> x4, starting transfers between devices: 20.4 us -> 13.6 us  [exchange(): return lax.all_to_all(value, axes, 0, 0, tiled=True)]
    dot_general x8, matrix products: 5.88 us -> 8.8 us  [dot(): lax.dot_general(a, b, (contract, ((), ())), precision=precision, preferre...]
  transfers between devices with their start and end apart: 21 -> 18, of which waited for: 11 -> 11; matrix products, arithmetic and copies ran while one was open for 29% -> 8% of each run, Pallas kernels for 14% -> 17%
where the time goes in v1:
time: 210 us; the launch traced here: 208 us
  waiting for transfers between devices  72.3 us (34%)
  Pallas kernels  63.5 us (30%)
  starting transfers between devices  33.5 us (16%)
  blocking collectives  11.9 us (6%)
  matrix products  9.99 us (5%)
  local copies, waits for them, and re-layouts  8.88 us (4%)
  other arithmetic  7.5 us (4%)
    ppermute x3, waiting for transfers between devices, on_device(): block = lax.ppermute(block, 'rank', [(i, i ^ offset) for i in range(ranks)])  22.1 us
    ppermute x10, waiting for transfers between devices, swap(): return lax.ppermute(value, axis, pairs)  21.6 us
    pallas_call x2, Pallas kernels, invert_factor(): call(factor_kernel, 4 * gram.size * gram.shape[0], 8 * gram.size, out_sha...  15.5 us
    all_to_all x4, waiting for transfers between devices, exchange(): return lax.all_to_all(value, axes, 0, 0, tiled=True)  14.9 us
    all_to_all x1, waiting for transfers between devices, split_blocks(): lax.all_to_all(blocks, ('cuts', 'rank'), 0, 0, axis_index_groups=groups,...  13.7 us
    all_to_all x4, starting transfers between devices, exchange(): return lax.all_to_all(value, axes, 0, 0, tiled=True)  13.6 us
    pallas_call x1, Pallas kernels, square_of(): call(square_kernel, 4 * rows * width * width, 4 * flat_one.size, grid=(10...  13.4 us
    ppermute x10, starting transfers between devices, swap(): return lax.ppermute(value, axis, pairs)  12.8 us
  transfers between devices with their start and end apart: 18, of which 11 were waited for; matrix products, arithmetic and copies ran while one was open for 8% of the time, Pallas kernels for 17%

profile of v1, /device:TPU:0, one launch (start us, length us, event | category | flops | bytes accessed | tf_op | source)
XLA Modules:
  0.0 208.5 jit_solution(3101848698760414839)
XLA Ops:
  0.6 13.4 %shard_map.68 = f32[512,512]{1,0:T(8,128)} custom-call(f32[5120,512]{1,0:T(8,128)} %bitcast.59), custom_call_target="tpu_custom_call" | custom-call | flops 5368709120 | bytes 10485760 | tf_op jit(solution)/shard_map/pallas_call | solution.py:120
  14.0 1.9 constant_dynamic-slice_fusion.9
  15.9 0.5 collective-permute-start
  16.3 10.9 %shard_map.67 = (f32[40,128,128]{2,1,0:T(8,128)}, f32[128,128]{1,0:T(8,128)}) custom-call(f32[128,40,512]{2,1,0:T(8,128)} %core_ref.3, f32[512,128]{1,0:T(8,128)} %right_ref.1, f32[128,40,128]{2,1,0:T(8,128)} %left_ref.1), custom_call_target="tpu_custom_call" | custom-call | flops 2684354560 | bytes 15728640 | tf_op jit(solution)/shard_map/pallas_call | solution.py:80
  27.2 11.9 %all_to_all.30 = f32[8,16,128]{2,1,0:T(8,128)S(1)} all-to-all(f32[8,16,128]{2,1,0:T(8,128)} %bitcast.78), channel_id=1, replica_groups=mesh['cuts'=8,'rank'=4] {'cuts'}, dimensions={0} | all-to-all | bytes 131072 | tf_op jit(solution)/shard_map/all_to_all | solution.py:276
  39.2 0.7 broadcast_in_dim.10
  39.9 3.1 %all-to-all-start.1 = ((f32[32,16,128]{2,1,0:T(8,128)}), f32[32,16,128]{2,1,0:T(8,128)S(1)}, u32[]{:S(2)}, u32[]{:S(2)}) async-start(f32[32,16,128]{2,1,0:T(8,128)} %broadcast_in_dim.10), calls=%async_computation.1 | async-start | bytes 524288 | tf_op jit(solution)/shard_map/all_to_all | solution.py:276
  43.0 1.9 add_bitcast_fusion
  45.0 9.0 %all-to-all-done.1 = f32[32,16,128]{2,1,0:T(8,128)S(1)} async-done(((f32[32,16,128]{2,1,0:T(8,128)}), f32[32,16,128]{2,1,0:T(8,128)S(1)}, u32[]{:S(2)}, u32[]{:S(2)}) %all-to-all-start.1) | async-done | bytes 262176 | tf_op jit(solution)/shard_map/all_to_all | solution.py:276
  54.0 3.6 %all-to-all-start.2 = ((f32[16,16,512]{2,1,0:T(8,128)}), f32[16,16,512]{2,1,0:T(8,128)S(1)}, u32[]{:S(2)}, u32[]{:S(2)}) async-start(f32[16,16,512]{2,1,0:T(8,128)} %add_bitcast_fusion), calls=%async_computation.2 | async-start | bytes 1048576 | tf_op jit(solution)/shard_map/all_to_all | solution.py:280
  57.6 1.0 copy.12
  58.5 13.7 %all-to-all-done.2 = f32[16,16,512]{2,1,0:T(8,128)S(1)} async-done(((f32[16,16,512]{2,1,0:T(8,128)}), f32[16,16,512]{2,1,0:T(8,128)S(1)}, u32[]{:S(2)}, u32[]{:S(2)}) %all-to-all-start.2) | async-done | bytes 524320 | tf_op jit(solution)/shard_map/all_to_all | solution.py:280
  72.3 0.2 fusion.1
  72.6 0.7 broadcast_in_dim.11
  73.3 3.0 %all-to-all-start.3 = ((f32[32,16,128]{2,1,0:T(8,128)}), f32[32,16,128]{2,1,0:T(8,128)S(1)}, u32[]{:S(2)}, u32[]{:S(2)}) async-start(f32[32,16,128]{2,1,0:T(8,128)} %broadcast_in_dim.11), calls=%async_computation.3 | async-start | bytes 524288 | tf_op jit(solution)/shard_map/all_to_all | solution.py:276
  76.4 1.5 constant_dynamic-slice_fusion.1
  77.9 2.5 %collective-permute-start.3 = (f32[10,128,128]{2,1,0:T(8,128)}, f32[10,128,128]{2,1,0:T(8,128)S(1)}, u32[]{:S(2)}, u32[]{:S(2)}) collective-permute-start(f32[10,128,128]{2,1,0:T(8,128)} %get-tuple-element.15), channel_id=1, source_target_pairs={{0,3},{1,2},{2,1},{3,0},{4,7},{5,6},{6,5},{7,4},{8,11},{9,10},{10,... | collective-permute-start | bytes 1966088 | tf_op jit(solution)/shard_map/ppermute | solution.py:390
  80.4 0.6 collective-permute-start.2
  81.0 0.4 collective-permute-start.1
  81.4 5.9 %all-to-all-done.3 = f32[32,16,128]{2,1,0:T(8,128)S(1)} async-done(((f32[32,16,128]{2,1,0:T(8,128)}), f32[32,16,128]{2,1,0:T(8,128)S(1)}, u32[]{:S(2)}, u32[]{:S(2)}) %all-to-all-start.3) | async-done | bytes 262176 | tf_op jit(solution)/shard_map/all_to_all | solution.py:276
  87.3 0.7 pad_maximum_fusion.4.raw_ref
  88.0 1.2 fusion.2.gram_ref
  89.2 8.6 %collective-permute-done.3.refs_3_ = f32[10,128,128]{2,1,0:T(8,128)S(1)} collective-permute-done((f32[10,128,128]{2,1,0:T(8,128)}, f32[10,128,128]{2,1,0:T(8,128)S(1)}, u32[]{:S(2)}, u32[]{:S(2)}) %collective-permute-start.3) | collective-permute-done | bytes 655392 | tf_op jit(solution)/shard_map/ppermute | solution.py:390
  97.8 13.6 %collective-permute-done.2.refs_2_ = f32[10,128,128]{2,1,0:T(8,128)S(1)} collective-permute-done((f32[10,128,128]{2,1,0:T(8,128)}, f32[10,128,128]{2,1,0:T(8,128)S(1)}, u32[]{:S(2)}, u32[]{:S(2)}) %collective-permute-start.2) | collective-permute-done | bytes 655392 | tf_op jit(solution)/shard_map/ppermute | solution.py:390
  111.4 0.8 copy-done.5
  112.2 0.2 copy-done.6
  112.4 4.2 %shard_map.69 = f32[10,128,128]{2,1,0:T(8,128)} custom-call(f32[512,128]{1,0:T(8,128)} %pad_maximum_fusion.4.raw_ref, f32[10,128,128]{2,1,0:T(8,128)} %get-tuple-element.18.refs_0_, f32[10,128,128]{2,1,0:T(8,128)} %copy-done.6, f32[10,128,128]{2,1,0:T(8,128)} %copy-done.5, f32[10,128,128]{2,1,0:T(8,128)} %copy-done.4), custom_call_target="tpu_custom_call" | custom-call | flops 671088640 | bytes 2883584 | tf_op jit(solution)/shard_map/pallas_call | solution.py:143
  116.6 1.1 slice_bitcast_fusion.1
  117.8 1.2 collective-permute-start.4
  119.0 0.6 collective-permute-start.6
  119.6 7.8 %shard_map.70 = f32[128,128]{1,0:T(8,128)} custom-call(f32[128,128]{1,0:T(8,128)} %fusion.2.gram_ref), custom_call_target="tpu_custom_call" | custom-call | flops 8388608 | bytes 131072 | tf_op jit(solution)/shard_map/pallas_call | solution.py:350
  127.3 1.1 fusion.3
  128.5 1.2 broadcast_select_fusion.7
  129.8 1.5 collective-permute-start.7
  131.3 1.0 collective-permute-start.5
  132.3 0.2 fusion.4
  132.5 0.6 pad_maximum_fusion.5.weight_ref
  133.1 1.2 convolution_bitcast_fusion
  134.3 11.4 %collective-permute-done.7 = f32[2,5,128,128]{3,2,1,0:T(8,128)S(1)} collective-permute-done((f32[2,5,128,128]{3,2,1,0:T(8,128)S(1)}, f32[2,5,128,128]{3,2,1,0:T(8,128)S(1)}, u32[]{:S(2)}, u32[]{:S(2)}) %collective-permute-start.7) | collective-permute-done | bytes 655392 | tf_op jit(solution)/shard_map/ppermute | solution.py:235
  145.7 1.5 collective-permute-done.5
  147.2 0.2 broadcast_select_fusion.1
  147.4 0.1 pad_maximum_fusion.1
  147.6 0.1 copy.14
  147.6 1.8 pad_maximum_fusion
  149.4 10.9 %shard_map.72 = (f32[512,128]{1,0:T(8,128)}, f32[32,40,128]{2,1,0:T(8,128)}) custom-call(f32[40,128,128]{2,1,0:T(8,128)} %bitcast.61, f32[160,128]{1,0:T(8,128)} %pad_maximum_fusion.5.weight_ref, f32[128,40,512]{2,1,0:T(8,128)} %core_ref.3), custom_call_target="tpu_custom_call" | custom-call | flops 2684354560 | bytes 13107200 | tf_op jit(solution)/shard_map/pallas_call | solution.py:183
  160.3 4.2 %all-to-all-start.4 = ((f32[32,16,128]{2,1,0:T(8,128)}), f32[32,16,128]{2,1,0:T(8,128)S(1)}, u32[]{:S(2)}, u32[]{:S(2)}) async-start(f32[32,16,128]{2,1,0:T(8,128)} %bitcast.77), calls=%async_computation.4 | async-start | bytes 524288 | tf_op jit(solution)/shard_map/all_to_all | solution.py:276
  164.5 0.7 convolution_bitcast_fusion.1
  165.2 0.1 collective-permute-start.8
  165.3 1.2 collective-permute-done.8
  166.6 1.6 collective-permute-start.9
  168.2 3.2 %collective-permute-done.9 = f32[128,128]{1,0:T(8,128)S(1)} collective-permute-done((f32[128,128]{1,0:T(8,128)S(1)}, f32[128,128]{1,0:T(8,128)S(1)}, u32[]{:S(2)}, u32[]{:S(2)}) %collective-permute-start.9) | collective-permute-done | bytes 65568 | tf_op jit(solution)/shard_map/ppermute | solution.py:235
  171.4 1.6 collective-permute-start.10
  173.0 2.8 %collective-permute-done.10 = f32[128,128]{1,0:T(8,128)S(1)} collective-permute-done((f32[128,128]{1,0:T(8,128)S(1)}, f32[128,128]{1,0:T(8,128)S(1)}, u32[]{:S(2)}, u32[]{:S(2)}) %collective-permute-start.10) | collective-permute-done | bytes 65568 | tf_op jit(solution)/shard_map/ppermute | solution.py:235
  175.9 1.8 collective-permute-start.11
  177.7 1.1 convolution_multiply_fusion.1.weight_ref
  178.7 1.4 collective-permute-done.11
  180.2 3.0 %collective-permute-start.12 = (f32[128,128]{1,0:T(8,128)S(1)}, f32[128,128]{1,0:T(8,128)S(1)}, u32[]{:S(2)}, u32[]{:S(2)}) collective-permute-start(f32[128,128]{1,0:T(8,128)S(1)} %add.68), channel_id=1, source_target_pairs={{0,16},{4,20},{8,24},{12,28},{16,0},{20,4},{24,8},{28,12},{1,17},{... | collective-permute-start | bytes 196616 | tf_op jit(solution)/shard_map/ppermute | solution.py:235
  183.2 0.7 broadcast_in_dim.28
  183.9 3.3 %all-to-all-start.5 = ((f32[32,16,128]{2,1,0:T(8,128)}), f32[32,16,128]{2,1,0:T(8,128)S(1)}, u32[]{:S(2)}, u32[]{:S(2)}) async-start(f32[32,16,128]{2,1,0:T(8,128)} %broadcast_in_dim.28), calls=%async_computation.5 | async-start | bytes 524288 | tf_op jit(solution)/shard_map/all_to_all | solution.py:276
  187.2 8.6 %shard_map.71 = f32[5120,128]{1,0:T(8,128)} custom-call(f32[5120,512]{1,0:T(8,128)} %bitcast.60, f32[512,128]{1,0:T(8,128)} %convolution_multiply_fusion.1.weight_ref), custom_call_target="tpu_custom_call" | custom-call | flops 2684354560 | bytes 13107200 | tf_op jit(solution)/shard_map/pallas_call | solution.py:214
  195.8 0.6 add.69.gram_ref
  196.5 7.7 %shard_map.73 = f32[128,128]{1,0:T(8,128)} custom-call(f32[128,128]{1,0:T(8,128)} %add.69.gram_ref), custom_call_target="tpu_custom_call" | custom-call | flops 8388608 | bytes 131072 | tf_op jit(solution)/shard_map/pallas_call | solution.py:350
  204.2 2.4 %convolution_multiply_fusion = f32[1280,128]{1,0:T(8,128)} fusion(f32[1280,128]{1,0:T(8,128)S(1)} %bitcast.75, f32[128,128]{1,0:T(8,128)} %shard_map.73), kind=kOutput, calls=%fused_computation.1 | convolution fusion | flops 251822080 | bytes 1376256 | tf_op jit(solution)/shard_map/dot_general | solution.py:359
  206.6 1.9 fusion.5
  (33 shorter events, 0.3 us)
Async XLA Ops:
  15.9 27.2 %collective-permute-start = (f32[1,16,16,512]{3,2,1,0:T(8,128)}, f32[1,16,16,512]{3,2,1,0:T(8,128)S(1)}, u32[]{:S(2)}, u32[]{:S(2)}) collective-permute-start(f32[1,16,16,512]{3,2,1,0:T(8,128)} %constant_dynamic-slice_fusion.9), channel_id=1, source_target_pairs={{0,4},{4,0},{8,12},{12,8},{16,20},{20,16},{24,28},{28,24},{1,5},{5... | collective-permute-start | bytes 1572872 | tf_op jit(solution)/shard_map/ppermute | solution.py:235
  39.9 36.5 %copy-start.1 = (f32[40,128,128]{2,1,0:T(8,128)S(1)}, f32[40,128,128]{2,1,0:T(8,128)}, u32[]{:S(2)}) copy-start(f32[40,128,128]{2,1,0:T(8,128)} %get-tuple-element.10) | copy-start | bytes 7864324
  39.9 14.1 %all-to-all-start.1 = ((f32[32,16,128]{2,1,0:T(8,128)}), f32[32,16,128]{2,1,0:T(8,128)S(1)}, u32[]{:S(2)}, u32[]{:S(2)}) async-start(f32[32,16,128]{2,1,0:T(8,128)} %broadcast_in_dim.10), calls=%async_computation.1 | async-start | bytes 524288 | tf_op jit(solution)/shard_map/all_to_all | solution.py:276
  54.0 3.6 %copy-start.3 = (f32[32,16,128]{2,1,0:T(8,128)}, f32[32,16,128]{2,1,0:T(8,128)S(1)}, u32[]{:S(2)}) copy-start(f32[32,16,128]{2,1,0:T(8,128)S(1)} %all-to-all-done.1) | copy-start | bytes 786436
  54.0 18.3 %all-to-all-start.2 = ((f32[16,16,512]{2,1,0:T(8,128)}), f32[16,16,512]{2,1,0:T(8,128)S(1)}, u32[]{:S(2)}, u32[]{:S(2)}) async-start(f32[16,16,512]{2,1,0:T(8,128)} %add_bitcast_fusion), calls=%async_computation.2 | async-start | bytes 1048576 | tf_op jit(solution)/shard_map/all_to_all | solution.py:280
  73.3 14.0 %all-to-all-start.3 = ((f32[32,16,128]{2,1,0:T(8,128)}), f32[32,16,128]{2,1,0:T(8,128)S(1)}, u32[]{:S(2)}, u32[]{:S(2)}) async-start(f32[32,16,128]{2,1,0:T(8,128)} %broadcast_in_dim.11), calls=%async_computation.3 | async-start | bytes 524288 | tf_op jit(solution)/shard_map/all_to_all | solution.py:276
  77.9 19.9 %collective-permute-start.3 = (f32[10,128,128]{2,1,0:T(8,128)}, f32[10,128,128]{2,1,0:T(8,128)S(1)}, u32[]{:S(2)}, u32[]{:S(2)}) collective-permute-start(f32[10,128,128]{2,1,0:T(8,128)} %get-tuple-element.15), channel_id=1, source_target_pairs={{0,3},{1,2},{2,1},{3,0},{4,7},{5,6},{6,5},{7,4},{8,11},{9,10},{10,... | collective-permute-start | bytes 1966088 | tf_op jit(solution)/shard_map/ppermute | solution.py:390
  80.4 31.0 %collective-permute-start.2 = (f32[10,128,128]{2,1,0:T(8,128)}, f32[10,128,128]{2,1,0:T(8,128)S(1)}, u32[]{:S(2)}, u32[]{:S(2)}) collective-permute-start(f32[10,128,128]{2,1,0:T(8,128)} %get-tuple-element.16), channel_id=1, source_target_pairs={{0,2},{1,3},{2,0},{3,1},{4,6},{5,7},{6,4},{7,5},{8,10},{9,11},{10,... | collective-permute-start | bytes 1966088 | tf_op jit(solution)/shard_map/ppermute | solution.py:390
  81.0 30.4 %collective-permute-start.1 = (f32[10,128,128]{2,1,0:T(8,128)}, f32[10,128,128]{2,1,0:T(8,128)S(1)}, u32[]{:S(2)}, u32[]{:S(2)}) collective-permute-start(f32[10,128,128]{2,1,0:T(8,128)} %get-tuple-element.17), channel_id=1, source_target_pairs={{0,1},{1,0},{2,3},{3,2},{4,5},{5,4},{6,7},{7,6},{8,9},{9,8},{10,11... | collective-permute-start | bytes 1966088 | tf_op jit(solution)/shard_map/ppermute | solution.py:390
  97.8 13.6 %copy-start.4 = (f32[10,128,128]{2,1,0:T(8,128)}, f32[10,128,128]{2,1,0:T(8,128)S(1)}, u32[]{:S(2)}) copy-start(f32[10,128,128]{2,1,0:T(8,128)S(1)} %collective-permute-done.3.refs_3_) | copy-start | bytes 1966084
  111.4 0.8 copy-start.5
  111.4 1.0 copy-start.6
  117.8 10.7 %collective-permute-start.4 = (f32[1,5,128,128]{3,2,1,0:T(8,128)S(1)}, f32[1,5,128,128]{3,2,1,0:T(8,128)S(1)}, u32[]{:S(2)}, u32[]{:S(2)}) collective-permute-start(f32[1,5,128,128]{3,2,1,0:T(8,128)S(1)} %get-tuple-element.29), channel_id=1, source_target_pairs={{0,1},{1,0},{2,3},{3,2},{4,5},{5,4},{6,7},{7,6},{8,9},{9,8},{10,11... | collective-permute-start | bytes 983048 | tf_op jit(solution)/shard_map/ppermute | solution.py:235
  119.0 9.5 %collective-permute-start.6 = (f32[1,5,128,128]{3,2,1,0:T(8,128)S(1)}, f32[1,5,128,128]{3,2,1,0:T(8,128)S(1)}, u32[]{:S(2)}, u32[]{:S(2)}) collective-permute-start(f32[1,5,128,128]{3,2,1,0:T(8,128)S(1)} %get-tuple-element.30), channel_id=1, source_target_pairs={{0,2},{1,3},{2,0},{3,1},{4,6},{5,7},{6,4},{7,5},{8,10},{9,11},{10,... | collective-permute-start | bytes 983048 | tf_op jit(solution)/shard_map/ppermute | solution.py:235
  128.4 3.8 %copy-start.2 = (f32[128,128]{1,0:T(8,128)S(1)}, f32[128,128]{1,0:T(8,128)}, u32[]{:S(2)}) copy-start(f32[128,128]{1,0:T(8,128)} %shard_map.70) | copy-start | bytes 196612
  128.5 4.7 %copy-start = (f32[10,128,128]{2,1,0:T(8,128)S(1)}, f32[10,128,128]{2,1,0:T(8,128)}, u32[]{:S(2)}) copy-start(f32[10,128,128]{2,1,0:T(8,128)} %shard_map.69) | copy-start | bytes 1966084
  129.8 15.9 %collective-permute-start.7 = (f32[2,5,128,128]{3,2,1,0:T(8,128)S(1)}, f32[2,5,128,128]{3,2,1,0:T(8,128)S(1)}, u32[]{:S(2)}, u32[]{:S(2)}) collective-permute-start(f32[2,5,128,128]{3,2,1,0:T(8,128)S(1)} %pad_maximum_fusion.3), channel_id=1, source_target_pairs={{0,1},{1,0},{2,3},{3,2},{4,5},{5,4},{6,7},{7,6},{8,9},{9,8},{10,11... | collective-permute-start | bytes 1966088 | tf_op jit(solution)/shard_map/ppermute | solution.py:235
  131.3 15.9 %collective-permute-start.5 = (f32[2,5,128,128]{3,2,1,0:T(8,128)S(1)}, f32[2,5,128,128]{3,2,1,0:T(8,128)S(1)}, u32[]{:S(2)}, u32[]{:S(2)}) collective-permute-start(f32[2,5,128,128]{3,2,1,0:T(8,128)S(1)} %pad_maximum_fusion.2), channel_id=1, source_target_pairs={{0,2},{1,3},{2,0},{3,1},{4,6},{5,7},{6,4},{7,5},{8,10},{9,11},{10,... | collective-permute-start | bytes 1966088 | tf_op jit(solution)/shard_map/ppermute | solution.py:235
  160.3 22.9 %all-to-all-start.4 = ((f32[32,16,128]{2,1,0:T(8,128)}), f32[32,16,128]{2,1,0:T(8,128)S(1)}, u32[]{:S(2)}, u32[]{:S(2)}) async-start(f32[32,16,128]{2,1,0:T(8,128)} %bitcast.77), calls=%async_computation.4 | async-start | bytes 524288 | tf_op jit(solution)/shard_map/all_to_all | solution.py:276
  165.2 1.3 collective-permute-start.8
  166.6 4.9 %collective-permute-start.9 = (f32[128,128]{1,0:T(8,128)S(1)}, f32[128,128]{1,0:T(8,128)S(1)}, u32[]{:S(2)}, u32[]{:S(2)}) collective-permute-start(f32[128,128]{1,0:T(8,128)S(1)} %add.65), channel_id=1, source_target_pairs={{0,1},{1,0},{2,3},{3,2},{4,5},{5,4},{6,7},{7,6},{8,9},{9,8},{10,11... | collective-permute-start | bytes 196616 | tf_op jit(solution)/shard_map/ppermute | solution.py:235
  171.4 4.4 %collective-permute-start.10 = (f32[128,128]{1,0:T(8,128)S(1)}, f32[128,128]{1,0:T(8,128)S(1)}, u32[]{:S(2)}, u32[]{:S(2)}) collective-permute-start(f32[128,128]{1,0:T(8,128)S(1)} %add.66), channel_id=1, source_target_pairs={{0,2},{1,3},{2,0},{3,1},{4,6},{5,7},{6,4},{7,5},{8,10},{9,11},{10,... | collective-permute-start | bytes 196616 | tf_op jit(solution)/shard_map/ppermute | solution.py:235
  175.9 4.3 %collective-permute-start.11 = (f32[128,128]{1,0:T(8,128)S(1)}, f32[128,128]{1,0:T(8,128)S(1)}, u32[]{:S(2)}, u32[]{:S(2)}) collective-permute-start(f32[128,128]{1,0:T(8,128)S(1)} %add.67), channel_id=1, source_target_pairs={{0,8},{4,12},{8,0},{12,4},{16,24},{20,28},{24,16},{28,20},{1,9},{5... | collective-permute-start | bytes 196616 | tf_op jit(solution)/shard_map/ppermute | solution.py:235
  180.2 15.6 %collective-permute-start.12 = (f32[128,128]{1,0:T(8,128)S(1)}, f32[128,128]{1,0:T(8,128)S(1)}, u32[]{:S(2)}, u32[]{:S(2)}) collective-permute-start(f32[128,128]{1,0:T(8,128)S(1)} %add.68), channel_id=1, source_target_pairs={{0,16},{4,20},{8,24},{12,28},{16,0},{20,4},{24,8},{28,12},{1,17},{... | collective-permute-start | bytes 196616 | tf_op jit(solution)/shard_map/ppermute | solution.py:235
  183.9 22.6 %all-to-all-start.5 = ((f32[32,16,128]{2,1,0:T(8,128)}), f32[32,16,128]{2,1,0:T(8,128)S(1)}, u32[]{:S(2)}, u32[]{:S(2)}) async-start(f32[32,16,128]{2,1,0:T(8,128)} %broadcast_in_dim.28), calls=%async_computation.5 | async-start | bytes 524288 | tf_op jit(solution)/shard_map/all_to_all | solution.py:276
  187.2 17.0 %copy-start.7 = (f32[32,40,128]{2,1,0:T(8,128)S(1)}, f32[32,40,128]{2,1,0:T(8,128)}, u32[]{:S(2)}) copy-start(f32[32,40,128]{2,1,0:T(8,128)} %get-tuple-element.13) | copy-start | bytes 1966084
